TPU v7x, 32 devices: a whole 2x2x4 slice. The times are simulated.
32 devices in a mesh: atom: 16 (over z, y, core), aux: 2 (over x).
Axes of the slice: x: 2, y: 2, z: 4, core: 2. Of those that a mesh axis runs over, the one named last changes fastest.
Arguments:
- three: bfloat16 [32, 128, 128, 384], P('atom', 'aux'), may hold values from -0.5 to 0.5
- occupied: bfloat16 [4096, 384], P(('atom', 'aux')), may hold values from -0.3125 to 0.3125
- virtual: bfloat16 [4096, 384], P(('atom', 'aux')), may hold values from -0.3125 to 0.3125
- three_mask: int32 [32, 3], replicated, may hold values from 0 to 1, as said below
- occ_mask: int32 [32, 3], replicated, may hold values from 0 to 1, as said below
- vir_mask: int32 [32, 3], replicated, may hold values from 0 to 1, as said below
- atom_sizes: int32 [32], replicated, may hold values from 64 to 128
Outputs:
- polarizability: float32 [32, 128, 384], P('atom', 'aux')
Inputs may be any that keep to these rules, and one draw needn't show every extreme that they name: three_mask[b, 1] = 1 for every block b; the slab pairs its atom blocks into molecules of two, and every block keeps its tile towards the neighbouring molecule: three_mask[b, 0] = 1 for even b and three_mask[b, 2] = 1 for odd b. occ_mask[b, 1] = 1 for every block b; occ_mask[b, 0] = 1 where b is a multiple of 2, and occ_mask[b, 2] = 1 where b + 1 is a multiple of 2. vir_mask[b, 1] = 1 for every block b.
All inputs are finite; a program needn't handle non-finite values.
Results may differ from a plain program's by a relative error of at most 0.0041.
Values may be sent and summed in bfloat16 or wider, within the bound.
A program may use at most 320 MiB of HBM per device.

v0:
```python
import jax
import jax.numpy as jnp
from jax import lax
from jax.sharding import PartitionSpec as P


def with_halo(cells, sides, width):
    for axis, dim in sides:
        count = lax.axis_size(axis)
        head = lax.slice_in_dim(cells, 0, width, axis=dim)
        tail = lax.slice_in_dim(cells, cells.shape[dim] - width, cells.shape[dim], axis=dim)
        cells = jnp.concatenate(
            [
                lax.ppermute(tail, axis, [(i, (i + 1) % count) for i in range(count)]),
                cells,
                lax.ppermute(head, axis, [((i + 1) % count, i) for i in range(count)]),
            ],
            axis=dim,
        )
    return cells


def from_behind(value, axis, steps):
    count = lax.axis_size(axis)
    pairs = [(source, (source + steps) % count) for source in range(count)]
    return lax.ppermute(value, axis, pairs)


def pick_sizes(lookup, blocks):
    matches = blocks[:, None] == jnp.arange(lookup.shape[0], dtype=jnp.int32)[None, :]
    return jnp.sum(jnp.where(matches, lookup[None, :], 0), axis=1)


def pick_rows(lookup, blocks):
    matches = blocks[:, None] == jnp.arange(lookup.shape[0], dtype=jnp.int32)[None, :]
    return jnp.sum(jnp.where(matches[:, :, None], lookup[None, :, :], 0), axis=1)


def block_ids(first_block, block_count, total_blocks):
    return (first_block + jnp.arange(block_count, dtype=jnp.int32) + total_blocks) % total_blocks


def band_live(atom_sizes, mask_table, blocks, block_width):
    total_blocks = atom_sizes.shape[0]
    block_count = blocks.shape[0]
    inside = jnp.arange(block_width, dtype=jnp.int32)
    partners = (
        blocks[:, None] + jnp.arange(3, dtype=jnp.int32)[None, :] + total_blocks - 1
    ) % total_blocks
    own_size = pick_sizes(atom_sizes, blocks)
    partner_size = pick_sizes(atom_sizes, partners.reshape(-1)).reshape(block_count, 3)
    live_blocks = pick_rows(mask_table, blocks) > 0
    row_ok = inside[None, :] < own_size[:, None]
    col_ok = inside[None, None, :] < partner_size[:, :, None]
    both = row_ok[:, :, None, None] & col_ok[:, None, :, :] & live_blocks[:, None, :, None]
    return both.reshape(block_count, block_width, 3 * block_width)


def block_live(mask_table, blocks, block_width):
    block_count = blocks.shape[0]
    live_blocks = pick_rows(mask_table, blocks) > 0
    spread = jnp.broadcast_to(
        live_blocks[:, None, :, None], (block_count, block_width, 3, block_width)
    )
    return spread.reshape(block_count * block_width, 3 * block_width)


def shards(three, occupied, virtual, three_mask, occ_mask, vir_mask, atom_sizes):
    zero_bf = jnp.zeros((), jnp.bfloat16)
    block_count = three.shape[0]
    aux_local = three.shape[1]
    block_width = three.shape[2]
    total_blocks = atom_sizes.shape[0]
    first_block = lax.axis_index("atom") * block_count
    local_ids = block_ids(first_block, block_count, total_blocks)
    band_ok = band_live(atom_sizes, three_mask, local_ids, block_width)
    coupling = jnp.where(band_ok[:, None], three, zero_bf)
    occ_rows, vir_rows = (
        lax.all_gather(occupied, "aux", axis=0, tiled=True),
        lax.all_gather(virtual, "aux", axis=0, tiled=True),
    )
    occ_live = jnp.where(block_live(occ_mask, local_ids, block_width), occ_rows, zero_bf)
    vir_live = jnp.where(block_live(vir_mask, local_ids, block_width), vir_rows, zero_bf)
    vir_ext = with_halo(vir_live, (("atom", 0),), block_width)
    mixed = None
    for offset in range(3):
        coupled = coupling[:, :, :, offset * block_width : (offset + 1) * block_width]
        partner_rows = vir_ext[offset * block_width : (offset + block_count) * block_width]
        partner_rows = partner_rows.reshape(block_count, block_width, 3 * block_width)
        product = jnp.einsum(
            "lpmb,lbc->lpmc", coupled, partner_rows, preferred_element_type=jnp.float32
        )
        padded = jnp.pad(
            product, ((0, 0), (0, 0), (0, 0), (offset * block_width, (2 - offset) * block_width))
        )
        mixed = padded if offset == 0 else mixed + padded
    mixed = mixed.astype(jnp.bfloat16)
    occ_tiles = occ_live.reshape(block_count, block_width, 3 * block_width)
    paired = []
    for target in range(3):
        density = occ_tiles[:, :, target * block_width : (target + 1) * block_width]
        screened = jnp.einsum(
            "lmj,lpmc->lpjc",
            density,
            mixed[:, :, :, target * block_width : (target + 3) * block_width],
            preferred_element_type=jnp.float32,
        )
        paired.append(screened.astype(jnp.bfloat16))
    from_left = from_behind(paired[2][-1], "atom", 1)
    from_right = from_behind(paired[0][0], "atom", -1)
    before = jnp.concatenate([from_left[None], paired[2][:-1]], axis=0)
    after = jnp.concatenate([paired[0][1:], from_right[None]], axis=0)
    sources = jnp.stack([before, paired[1], after], axis=1)
    total_aux = aux_local * lax.axis_size("aux")
    tile_sum = jnp.einsum(
        "lqrc,loprc->lqop",
        lax.all_gather(coupling, "aux", axis=1, tiled=True),
        sources,
        preferred_element_type=jnp.float32,
    )
    swapped = lax.all_to_all(tile_sum, "aux", split_axis=1, concat_axis=3, tiled=True)
    return swapped.reshape(block_count, aux_local, 3 * total_aux)


def solution(mesh):
    in_specs = (
        P("atom", "aux", None, None),
        P(("atom", "aux"), None),
        P(("atom", "aux"), None),
        P(),
        P(),
        P(),
        P(),
    )
    out_specs = P("atom", "aux", None)
    return jax.shard_map(shards, mesh=mesh, in_specs=in_specs, out_specs=out_specs, check_vma=False)
```

profile of v0, /device:TPU:0, one launch (start us, length us, event | category | flops | bytes accessed | tf_op | source)
XLA Modules:
  0.0 395.9 jit_solution(6158620312043457783)
XLA Ops:
  6.7 1.0 select_reduce_fusion.1
  8.0 0.8 select_reduce_fusion.4
  8.8 0.8 select_reduce_fusion
  10.0 10.5 %broadcast_select_fusion = bf16[2,64,128,384]{3,2,1,0:T(8,128)(2,1)} fusion(bf16[2,64,128,384]{3,2,1,0:T(8,128)(2,1)} %param.7, pred[2,128,384]{2,1,0:T(8,128)(4,1)S(1)} %and_and_fusion), kind=kLoop, calls=%fused_computation.15 | loop fusion | flops 6291456 | bytes 25264128 | tf_op jit(solution)/shard_map/jit(_where)/select_n | solution.py:77
  20.7 0.7 copy-done.1
  21.5 6.4 %all_gather.10 = bf16[256,384]{1,0:T(8,128)(2,1)S(1)} all-gather(bf16[128,384]{1,0:T(8,128)(2,1)S(1)} %copy-done.1), channel_id=1, replica_groups=mesh['atom'=16,'aux'=2] {'aux'}, dimensions={0}, use_global_device_ids=true | all-gather | bytes 294912 | tf_op jit(solution)/shard_map/all_gather | solution.py:80
  28.2 4.4 %collective-permute-start.1 = (bf16[128,384]{1,0:T(8,128)(2,1)S(1)}, bf16[128,384]{1,0:T(8,128)(2,1)S(1)}, u32[]{:S(2)}, u32[]{:S(2)}) collective-permute-start(bf16[128,384]{1,0:T(8,128)(2,1)S(1)} %get-tuple-element.15), channel_id=1, source_target_pairs={{2,0},{4,2},{6,4},{8,6},{10,8},{12,10},{14,12},{16,14},{18,16},{20... | collective-permute-start | bytes 294920 | tf_op jit(solution)/shard_map/ppermute | solution.py:16
  32.7 5.3 %all_gather.11 = bf16[256,384]{1,0:T(8,128)(2,1)S(1)} all-gather(bf16[128,384]{1,0:T(8,128)(2,1)S(1)} %copy-done.2), channel_id=1, replica_groups=mesh['atom'=16,'aux'=2] {'aux'}, dimensions={0}, use_global_device_ids=true | all-gather | bytes 294912 | tf_op jit(solution)/shard_map/all_gather | solution.py:79
  38.0 18.0 %fusion.16 = f32[2,64,128,384]{3,2,1,0:T(8,128)} fusion(bf16[2,128,384,1]{2,1,3,0:T(8,128)(2,1)S(1)} %bitcast.82, bf16[2,64,128,384]{3,2,1,0:T(8,128)(2,1)} %broadcast_select_fusion), kind=kOutput, calls=%fused_computation.20 | convolution fusion | flops 1610612736 | bytes 29556736 | tf_op jit(solution)/shard_map/lpmb,lbc->lpmc/dot_general | solution.py:90
  56.2 14.6 %fusion.14 = f32[2,64,128,384]{3,2,1,0:T(8,128)} fusion(bf16[2,128,384,1]{2,1,3,0:T(8,128)(2,1)S(1)} %bitcast.89, bf16[2,64,128,384]{3,2,1,0:T(8,128)(2,1)} %broadcast_select_fusion), kind=kOutput, calls=%fused_computation.18 | convolution fusion | flops 1610612736 | bytes 29556736 | tf_op jit(solution)/shard_map/lpmb,lbc->lpmc/dot_general | solution.py:90
  70.8 13.9 %fusion.18 = f32[2,64,128,384]{3,2,1,0:T(8,128)} fusion(bf16[2,128,384,1]{2,1,3,0:T(8,128)(2,1)S(1)} %bitcast.88, bf16[2,64,128,384]{3,2,1,0:T(8,128)(2,1)} %broadcast_select_fusion), kind=kOutput, calls=%fused_computation.22 | convolution fusion | flops 1610612736 | bytes 29556736 | tf_op jit(solution)/shard_map/lpmb,lbc->lpmc/dot_general | solution.py:90
  84.7 31.3 %add_convert_fusion = bf16[2,64,128,640]{3,2,1,0:T(8,128)(2,1)} fusion(f32[2,64,128,384]{3,2,1,0:T(8,128)} %fusion.14, f32[2,64,128,384]{3,2,1,0:T(8,128)} %fusion.16, f32[2,64,128,384]{3,2,1,0:T(8,128)} %fusion.18), kind=kLoop, calls=%fused_computation | loop fusion | flops 31457280 | bytes 96468992 | tf_op jit(solution)/shard_map/convert_element_type | solution.py:97
  116.0 10.5 %convert_bitcast_fusion.2 = bf16[2,64,128,384]{2,3,1,0:T(8,128)(2,1)} fusion(bf16[2,64,128,640]{3,2,1,0:T(8,128)(2,1)} %add_convert_fusion, bf16[2,128,384]{2,1,0:T(8,128)(2,1)S(1)} %bitcast.85), kind=kOutput, calls=%fused_computation.14 | convolution fusion | flops 1616904192 | bytes 25231360 | tf_op jit(solution)/shard_map/lmj,lpmc->lpjc/dot_general | solution.py:102
  126.5 9.7 %slice_bitcast_fusion.1 = (bf16[64,128,384]{1,2,0:T(8,128)(2,1)}, bf16[1,64,128,384]{2,3,1,0:T(8,128)(2,1)S(1)}) fusion(bf16[2,64,128,384]{2,3,1,0:T(8,128)(2,1)} %convert_bitcast_fusion.2), kind=kLoop, calls=%fused_computation.17 | loop fusion | bytes 25165824 | tf_op jit(solution)/shard_map/squeeze | solution.py:109
  136.2 10.5 %convert_bitcast_fusion = bf16[2,64,128,384]{2,3,1,0:T(8,128)(2,1)} fusion(bf16[2,64,128,640]{3,2,1,0:T(8,128)(2,1)} %add_convert_fusion, bf16[2,128,384]{2,1,0:T(8,128)(2,1)S(1)} %bitcast.86), kind=kOutput, calls=%fused_computation.12 | convolution fusion | flops 1616904192 | bytes 25231360 | tf_op jit(solution)/shard_map/lmj,lpmc->lpjc/dot_general | solution.py:102
  146.8 12.5 %fusion.25 = (bf16[1,64,128,384]{2,3,1,0:T(8,128)(2,1)}, bf16[64,128,384]{1,2,0:T(8,128)(2,1)}) fusion(bf16[2,64,128,384]{2,3,1,0:T(8,128)(2,1)} %convert_bitcast_fusion), kind=kLoop, calls=%fused_computation.58 | loop fusion | bytes 25165824 | tf_op jit(solution)/shard_map/slice | solution.py:112
  159.2 4.4 %collective-permute-start.3 = (bf16[64,128,384]{1,2,0:T(8,128)(2,1)}, bf16[64,128,384]{1,2,0:T(8,128)(2,1)}, u32[]{:S(2)}, u32[]{:S(2)}) collective-permute-start(bf16[64,128,384]{1,2,0:T(8,128)(2,1)} %get-tuple-element.11), channel_id=1, source_target_pairs={{0,30},{2,0},{4,2},{6,4},{8,6},{10,8},{12,10},{14,12},{16,14},{18,... | collective-permute-start | bytes 18874376 | tf_op jit(solution)/shard_map/ppermute | solution.py:26
  163.7 10.5 %convert_bitcast_fusion.1 = bf16[2,1,64,128,384]{3,4,2,0,1:T(8,128)(2,1)} fusion(bf16[2,64,128,640]{3,2,1,0:T(8,128)(2,1)} %add_convert_fusion, bf16[2,128,384]{2,1,0:T(8,128)(2,1)S(1)} %bitcast.87), kind=kOutput, calls=%fused_computation.13 | convolution fusion | flops 1616904192 | bytes 25231360 | tf_op jit(solution)/shard_map/lmj,lpmc->lpjc/dot_general | solution.py:102
  174.2 35.5 %collective-permute-done.2 = bf16[64,128,384]{1,2,0:T(8,128)(2,1)} collective-permute-done((bf16[64,128,384]{1,2,0:T(8,128)(2,1)}, bf16[64,128,384]{1,2,0:T(8,128)(2,1)}, u32[]{:S(2)}, u32[]{:S(2)}) %collective-permute-start.2) | collective-permute-done | bytes 6291488 | tf_op jit(solution)/shard_map/ppermute | solution.py:26
  209.7 9.2 %maximum_bitcast_fusion = bf16[2,1,64,128,384]{3,4,2,0,1:T(8,128)(2,1)} fusion(bf16[1,64,128,384]{2,3,1,0:T(8,128)(2,1)S(1)} %get-tuple-element.9, bf16[1,64,128,384]{2,3,1,0:T(8,128)(2,1)} %bitcast.16), kind=kLoop, calls=%fused_computation.10 | loop fusion | flops 6291456 | bytes 25165824 | tf_op jit(solution)/shard_map/stack | solution.py:113
  218.9 13.5 %collective-permute-done.3 = bf16[64,128,384]{1,2,0:T(8,128)(2,1)} collective-permute-done((bf16[64,128,384]{1,2,0:T(8,128)(2,1)}, bf16[64,128,384]{1,2,0:T(8,128)(2,1)}, u32[]{:S(2)}, u32[]{:S(2)}) %collective-permute-start.3) | collective-permute-done | bytes 6291488 | tf_op jit(solution)/shard_map/ppermute | solution.py:26
  232.5 8.3 %maximum_bitcast_fusion.1 = bf16[2,1,64,128,384]{3,4,2,0,1:T(8,128)(2,1)} fusion(bf16[1,64,128,384]{2,3,1,0:T(8,128)(2,1)} %bitcast.26, bf16[1,64,128,384]{2,3,1,0:T(8,128)(2,1)S(1)} %copy-done), kind=kLoop, calls=%fused_computation.11 | loop fusion | flops 6291456 | bytes 25165824 | tf_op jit(solution)/shard_map/stack | solution.py:113
  240.8 25.7 %pad_maximum_fusion = bf16[2,3,64,128,384]{3,4,2,0,1:T(8,128)(2,1)} fusion(bf16[2,1,64,128,384]{3,4,2,0,1:T(8,128)(2,1)} %maximum_bitcast_fusion.1, bf16[2,1,64,128,384]{3,4,2,0,1:T(8,128)(2,1)} %convert_bitcast_fusion.1, bf16[2,1,64,128,384]{3,4,2,0,1:T(8,128)(2,1)} %maximum_bitcast_fusion), kind=kLoop, calls=%fused_computation.1 | loop fusion | flops 37748736 | bytes 75497472 | tf_op jit(solution)/shard_map/stack | solution.py:113
  266.5 51.7 %all-gather.2.cloned.1.call-done = bf16[2,128,128,384]{3,2,1,0:T(8,128)(2,1)} async-done(((bf16[2,64,128,384]{3,2,1,0:T(8,128)(2,1)}), bf16[2,128,128,384]{3,2,1,0:T(8,128)(2,1)}) %all-gather.2.cloned.1.call-update) | async-done | bytes 25165840 | tf_op jit(solution)/shard_map/all_gather | solution.py:117
  318.2 32.1 %copy.65 = bf16[2,128,128,384,1]{2,1,3,4,0:T(8,128)(2,1)} copy(bf16[2,128,128,384,1]{3,2,1,0,4:T(8,128)(2,1)} %bitcast.81) | data formatting | bytes 50331648 | tf_op jit(solution)/shard_map/all_gather | solution.py:117
  350.3 27.3 %fusion.20 = f32[2,128,3,64]{1,3,2,0:T(8,128)S(1)} fusion(bf16[2,128,128,384,1]{2,1,3,4,0:T(8,128)(2,1)} %copy.65, bf16[2,3,64,128,384]{3,4,2,0,1:T(8,128)(2,1)} %pad_maximum_fusion), kind=kOutput, calls=%fused_computation.24 | convolution fusion | flops 4831838208 | bytes 63111168 | tf_op jit(solution)/shard_map/lqrc,loprc->lqop/dot_general | solution.py:115
  378.0 0.4 reshape.145
  378.4 7.2 %all_to_all.15 = f32[2,1,24576]{2,1,0:T(1,128)S(1)} all-to-all(f32[2,1,24576]{2,1,0:T(1,128)S(1)} %reshape.145), channel_id=1, replica_groups=mesh['atom'=16,'aux'=2] {'aux'}, dimensions={0} | all-to-all | bytes 393216 | tf_op jit(solution)/shard_map/all_to_all | solution.py:121
  385.6 0.5 broadcast.157
  386.1 1.2 reduce
  387.3 0.4 reshape.146
  388.0 1.0 reshape.136
  (37 shorter events, 2.2 us)
Async XLA Ops:
  6.5 311.7 %all-gather.2.cloned.1.call-start = ((), (), s32[]{:S(2)}) async-start(), calls=%async_computation.1 | async-start | bytes 37748736 | tf_op jit(solution)/shard_map/all_gather | solution.py:117
  20.6 0.9 copy-start.1
  20.6 12.1 %copy-start.2 = (bf16[128,384]{1,0:T(8,128)(2,1)S(1)}, bf16[128,384]{1,0:T(8,128)(2,1)}, u32[]{:S(2)}) copy-start(bf16[128,384]{1,0:T(8,128)(2,1)} %param.8) | copy-start | bytes 294916
  28.1 28.1 %collective-permute-start = (bf16[128,384]{1,0:T(8,128)(2,1)S(1)}, bf16[128,384]{1,0:T(8,128)(2,1)S(1)}, u32[]{:S(2)}, u32[]{:S(2)}) collective-permute-start(bf16[128,384]{1,0:T(8,128)(2,1)S(1)} %get-tuple-element.14), channel_id=1, source_target_pairs={{0,2},{2,4},{4,6},{6,8},{8,10},{10,12},{12,14},{14,16},{16,18},{18... | collective-permute-start | bytes 294920 | tf_op jit(solution)/shard_map/ppermute | solution.py:14
  28.2 28.0 %collective-permute-start.1 = (bf16[128,384]{1,0:T(8,128)(2,1)S(1)}, bf16[128,384]{1,0:T(8,128)(2,1)S(1)}, u32[]{:S(2)}, u32[]{:S(2)}) collective-permute-start(bf16[128,384]{1,0:T(8,128)(2,1)S(1)} %get-tuple-element.15), channel_id=1, source_target_pairs={{2,0},{4,2},{6,4},{8,6},{10,8},{12,10},{14,12},{16,14},{18,16},{20... | collective-permute-start | bytes 294920 | tf_op jit(solution)/shard_map/ppermute | solution.py:16
  136.2 73.5 %collective-permute-start.2 = (bf16[64,128,384]{1,2,0:T(8,128)(2,1)}, bf16[64,128,384]{1,2,0:T(8,128)(2,1)}, u32[]{:S(2)}, u32[]{:S(2)}) collective-permute-start(bf16[64,128,384]{1,2,0:T(8,128)(2,1)} %get-tuple-element.8), channel_id=1, source_target_pairs={{0,2},{2,4},{4,6},{6,8},{8,10},{10,12},{12,14},{14,16},{16,18},{18... | collective-permute-start | bytes 18874376 | tf_op jit(solution)/shard_map/ppermute | solution.py:26
  159.2 73.2 %collective-permute-start.3 = (bf16[64,128,384]{1,2,0:T(8,128)(2,1)}, bf16[64,128,384]{1,2,0:T(8,128)(2,1)}, u32[]{:S(2)}, u32[]{:S(2)}) collective-permute-start(bf16[64,128,384]{1,2,0:T(8,128)(2,1)} %get-tuple-element.11), channel_id=1, source_target_pairs={{0,30},{2,0},{4,2},{6,4},{8,6},{10,8},{12,10},{14,12},{16,14},{18,... | collective-permute-start | bytes 18874376 | tf_op jit(solution)/shard_map/ppermute | solution.py:26
  209.7 22.8 %copy-start = (bf16[1,64,128,384]{2,3,1,0:T(8,128)(2,1)S(1)}, bf16[1,64,128,384]{2,3,1,0:T(8,128)(2,1)}, u32[]{:S(2)}) copy-start(bf16[1,64,128,384]{2,3,1,0:T(8,128)(2,1)} %get-tuple-element.10) | copy-start | bytes 18874372
Sparse Core Ops, SparseCore 0:
  20.7 297.4 all-gather.1
where the time goes:
time: 397 us; the launch traced here: 396 us
  matrix products  105 us (26%)
  waiting for transfers between devices  101 us (25%)
  other arithmetic  89.5 us (23%)
  local copies, waits for them, and re-layouts  58.8 us (15%)
  blocking collectives  18.9 us (5%)
  between operations  13.5 us (3%)
  starting transfers between devices  8.93 us (2%)
    all_gather x1, waiting for transfers between devices, shards(): lax.all_gather(coupling, 'aux', axis=1, tiled=True)  51.7 us
    ppermute x2, waiting for transfers between devices, from_behind(): return lax.ppermute(value, axis, pairs)  49 us
    dot_general x3, matrix products, shards(): jnp.einsum('lpmb,lbc->lpmc', coupled, partner_rows, preferred_element_typ...  46.5 us
    another operation x3, other arithmetic, shards(): sources = jnp.stack([before, paired[1], after], axis=1)  43.2 us
    all_gather x1, local copies, waits for them, and re-layouts, shards(): lax.all_gather(coupling, 'aux', axis=1, tiled=True)  32.1 us
    dot_general x3, matrix products, shards(): jnp.einsum('lmj,lpmc->lpjc', density, mixed[:, :, :, target * block_width...  31.6 us
    convert_element_type x1, other arithmetic, shards(): mixed = mixed.astype(jnp.bfloat16)  31.3 us
    dot_general x1, matrix products, shards(): jnp.einsum('lqrc,loprc->lqop', lax.all_gather(coupling, 'aux', axis=1, ti...  27.3 us
  transfers between devices with their start and end apart: 5, of which 3 were waited for; matrix products, arithmetic and copies ran while one was open for 44% of the time, Pallas kernels for 0%

commit v1 on v0

--- a/solution.py
+++ b/solution.py
@@ -2,6 +2,18 @@
 import jax.numpy as jnp
 from jax import lax
 from jax.sharding import PartitionSpec as P
+
+
+def collect(x, axis, dim):
+    ways, here = (lax.axis_size(axis), lax.axis_index(axis))
+    grown, reach = (x, 1)
+    while reach < ways:
+        theirs = lax.ppermute(grown, axis, [(d, d ^ reach) for d in range(ways)])
+        mine_first = jnp.concatenate([grown, theirs], axis=dim)
+        theirs_first = jnp.concatenate([theirs, grown], axis=dim)
+        grown = jnp.where(here & reach == 0, mine_first, theirs_first)
+        reach = 2 * reach
+    return grown
 
 
 def with_halo(cells, sides, width):
@@ -113,10 +125,7 @@
     sources = jnp.stack([before, paired[1], after], axis=1)
     total_aux = aux_local * lax.axis_size("aux")
     tile_sum = jnp.einsum(
-        "lqrc,loprc->lqop",
-        lax.all_gather(coupling, "aux", axis=1, tiled=True),
-        sources,
-        preferred_element_type=jnp.float32,
+        "lqrc,loprc->lqop", collect(coupling, "aux", 1), sources, preferred_element_type=jnp.float32
     )
     swapped = lax.all_to_all(tile_sum, "aux", split_axis=1, concat_axis=3, tiled=True)
     return swapped.reshape(block_count, aux_local, 3 * total_aux)

time: 397 us -> 657 us (1.65)
  the two profiles are of different devices: /device:TPU:0 before, /device:TPU:20 now
where the time goes in v1:
time: 657 us; the launch traced here: 656 us
  blocking collectives  272 us (41%)
  other arithmetic  114 us (17%)
  waiting for transfers between devices  102 us (16%)
  matrix products  101 us (15%)
  local copies, waits for them, and re-layouts  61.3 us (9%)
    all_gather x1, blocking collectives, shards(): lax.all_gather(occupied, 'aux', axis=0, tiled=True)  259 us
    ppermute x2, waiting for transfers between devices, from_behind(): return lax.ppermute(value, axis, pairs)  102 us
    another operation x3, other arithmetic, shards(): sources = jnp.stack([before, paired[1], after], axis=1)  43.2 us
    dot_general x3, matrix products, shards(): jnp.einsum('lpmb,lbc->lpmc', coupled, partner_rows, preferred_element_typ...  41.8 us
    select_n x1, local copies, waits for them, and re-layouts, collect(): grown = jnp.where(here & reach == 0, mine_first, theirs_first)  32.2 us
    dot_general x3, matrix products, shards(): jnp.einsum('lmj,lpmc->lpjc', density, mixed[:, :, :, target * block_width...  31.9 us
    convert_element_type x1, other arithmetic, shards(): mixed = mixed.astype(jnp.bfloat16)  31.3 us
    dot_general x1, matrix products, shards(): jnp.einsum('lqrc,loprc->lqop', collect(coupling, 'aux', 1), sources, pref...  27.3 us
  transfers between devices with their start and end apart: 5, of which 1 were waited for; matrix products, arithmetic and copies ran while one was open for 28% of the time, Pallas kernels for 0%

profile of v1, /device:TPU:20, one launch (start us, length us, event | category | flops | bytes accessed | tf_op | source)
XLA Modules:
  0.0 655.9 jit_solution(16649537972283831874)
XLA Ops:
  0.1 1.0 select_reduce_fusion.1
  1.2 5.5 all_gather.6
  7.0 1.7 collective-permute-start.2
  9.1 0.8 select_reduce_fusion.4
  9.9 0.8 select_reduce_fusion
  11.2 10.6 %broadcast_select_fusion = bf16[2,64,128,384]{3,2,1,0:T(8,128)(2,1)} fusion(bf16[2,64,128,384]{3,2,1,0:T(8,128)(2,1)} %param.7, pred[2,128,384]{2,1,0:T(8,128)(4,1)S(1)} %and_and_fusion), kind=kLoop, calls=%fused_computation.17 | loop fusion | flops 6291456 | bytes 25264128 | tf_op jit(solution)/shard_map/jit(_where)/select_n | solution.py:89
  21.7 1.5 collective-permute-start
  23.2 14.0 %fusion.17 = f32[2,64,128,384]{3,2,1,0:T(8,128)} fusion(bf16[2,128,384,1]{2,1,3,0:T(8,128)(2,1)S(1)} %bitcast.84, bf16[2,64,128,384]{3,2,1,0:T(8,128)(2,1)} %broadcast_select_fusion), kind=kOutput, calls=%fused_computation.22 | convolution fusion | flops 1610612736 | bytes 29556736 | tf_op jit(solution)/shard_map/lpmb,lbc->lpmc/dot_general | solution.py:102
  37.3 258.9 %all_gather.7 = bf16[256,384]{1,0:T(8,128)(2,1)S(1)} all-gather(bf16[128,384]{1,0:T(8,128)(2,1)S(1)} %copy-done.1), channel_id=1, replica_groups=mesh['atom'=16,'aux'=2] {'aux'}, dimensions={0}, use_global_device_ids=true | all-gather | bytes 294912 | tf_op jit(solution)/shard_map/all_gather | solution.py:91
  296.5 13.9 %fusion.15 = f32[2,64,128,384]{3,2,1,0:T(8,128)} fusion(bf16[2,128,384,1]{2,1,3,0:T(8,128)(2,1)S(1)} %bitcast.91, bf16[2,64,128,384]{3,2,1,0:T(8,128)(2,1)} %broadcast_select_fusion), kind=kOutput, calls=%fused_computation.20 | convolution fusion | flops 1610612736 | bytes 29556736 | tf_op jit(solution)/shard_map/lpmb,lbc->lpmc/dot_general | solution.py:102
  310.4 13.9 %fusion.19 = f32[2,64,128,384]{3,2,1,0:T(8,128)} fusion(bf16[2,128,384,1]{2,1,3,0:T(8,128)(2,1)S(1)} %bitcast.90, bf16[2,64,128,384]{3,2,1,0:T(8,128)(2,1)} %broadcast_select_fusion), kind=kOutput, calls=%fused_computation.24 | convolution fusion | flops 1610612736 | bytes 29556736 | tf_op jit(solution)/shard_map/lpmb,lbc->lpmc/dot_general | solution.py:102
  324.3 31.3 %add_convert_fusion = bf16[2,64,128,640]{3,2,1,0:T(8,128)(2,1)} fusion(f32[2,64,128,384]{3,2,1,0:T(8,128)} %fusion.15, f32[2,64,128,384]{3,2,1,0:T(8,128)} %fusion.17, f32[2,64,128,384]{3,2,1,0:T(8,128)} %fusion.19), kind=kLoop, calls=%fused_computation | loop fusion | flops 31457280 | bytes 96468992 | tf_op jit(solution)/shard_map/convert_element_type | solution.py:109
  355.6 10.6 %convert_bitcast_fusion.2 = bf16[2,64,128,384]{2,3,1,0:T(8,128)(2,1)} fusion(bf16[2,64,128,640]{3,2,1,0:T(8,128)(2,1)} %add_convert_fusion, bf16[2,128,384]{2,1,0:T(8,128)(2,1)S(1)} %bitcast.87), kind=kOutput, calls=%fused_computation.16 | convolution fusion | flops 1616904192 | bytes 25231360 | tf_op jit(solution)/shard_map/lmj,lpmc->lpjc/dot_general | solution.py:114
  366.2 12.5 %slice_bitcast_fusion.1 = (bf16[64,128,384]{1,2,0:T(8,128)(2,1)}, bf16[1,64,128,384]{2,3,1,0:T(8,128)(2,1)}) fusion(bf16[2,64,128,384]{2,3,1,0:T(8,128)(2,1)} %convert_bitcast_fusion.2), kind=kLoop, calls=%fused_computation.19 | loop fusion | bytes 25165824 | tf_op jit(solution)/shard_map/squeeze | solution.py:121
  378.7 10.6 %convert_bitcast_fusion = bf16[2,64,128,384]{2,3,1,0:T(8,128)(2,1)} fusion(bf16[2,64,128,640]{3,2,1,0:T(8,128)(2,1)} %add_convert_fusion, bf16[2,128,384]{2,1,0:T(8,128)(2,1)S(1)} %bitcast.88), kind=kOutput, calls=%fused_computation.14 | convolution fusion | flops 1616904192 | bytes 25231360 | tf_op jit(solution)/shard_map/lmj,lpmc->lpjc/dot_general | solution.py:114
  389.3 12.8 %fusion.26 = (bf16[1,64,128,384]{2,3,1,0:T(8,128)(2,1)}, bf16[64,128,384]{1,2,0:T(8,128)(2,1)}) fusion(bf16[2,64,128,384]{2,3,1,0:T(8,128)(2,1)} %convert_bitcast_fusion), kind=kLoop, calls=%fused_computation.60 | loop fusion | bytes 25165824 | tf_op jit(solution)/shard_map/slice | solution.py:124
  402.1 1.7 collective-permute-start.4
  403.8 10.7 %convert_bitcast_fusion.1 = bf16[2,1,64,128,384]{3,4,2,0,1:T(8,128)(2,1)} fusion(bf16[2,64,128,640]{3,2,1,0:T(8,128)(2,1)} %add_convert_fusion, bf16[2,128,384]{2,1,0:T(8,128)(2,1)S(1)} %bitcast.89), kind=kOutput, calls=%fused_computation.15 | convolution fusion | flops 1616904192 | bytes 25231360 | tf_op jit(solution)/shard_map/lmj,lpmc->lpjc/dot_general | solution.py:114
  414.5 102.4 %collective-permute-done.3 = bf16[64,128,384]{1,2,0:T(8,128)(2,1)} collective-permute-done((bf16[64,128,384]{1,2,0:T(8,128)(2,1)}, bf16[64,128,384]{1,2,0:T(8,128)(2,1)}, u32[]{:S(2)}, u32[]{:S(2)}) %collective-permute-start.3) | collective-permute-done | bytes 6291488 | tf_op jit(solution)/shard_map/ppermute | solution.py:38
  516.9 9.2 %maximum_bitcast_fusion = bf16[2,1,64,128,384]{3,4,2,0,1:T(8,128)(2,1)} fusion(bf16[1,64,128,384]{2,3,1,0:T(8,128)(2,1)S(1)} %bitcast.83, bf16[1,64,128,384]{2,3,1,0:T(8,128)(2,1)} %bitcast.16), kind=kLoop, calls=%fused_computation.12 | loop fusion | flops 6291456 | bytes 25165824 | tf_op jit(solution)/shard_map/stack | solution.py:125
  526.1 8.3 %maximum_bitcast_fusion.1 = bf16[2,1,64,128,384]{3,4,2,0,1:T(8,128)(2,1)} fusion(bf16[1,64,128,384]{2,3,1,0:T(8,128)(2,1)} %bitcast.26, bf16[1,64,128,384]{2,3,1,0:T(8,128)(2,1)S(1)} %copy-done), kind=kLoop, calls=%fused_computation.13 | loop fusion | flops 6291456 | bytes 25165824 | tf_op jit(solution)/shard_map/stack | solution.py:125
  534.4 25.7 %pad_maximum_fusion = bf16[2,3,64,128,384]{3,4,2,0,1:T(8,128)(2,1)} fusion(bf16[2,1,64,128,384]{3,4,2,0,1:T(8,128)(2,1)} %maximum_bitcast_fusion.1, bf16[2,1,64,128,384]{3,4,2,0,1:T(8,128)(2,1)} %convert_bitcast_fusion.1, bf16[2,1,64,128,384]{3,4,2,0,1:T(8,128)(2,1)} %maximum_bitcast_fusion), kind=kLoop, calls=%fused_computation.1 | loop fusion | flops 37748736 | bytes 75497472 | tf_op jit(solution)/shard_map/stack | solution.py:125
  560.1 24.8 %fusion.2 = bf16[2,128,128,384,1]{3,2,1,0,4:T(8,128)(2,1)} fusion(bf16[2,64,128,384]{3,2,1,0:T(8,128)(2,1)} %collective-permute-done, bf16[2,64,128,384]{3,2,1,0:T(8,128)(2,1)} %broadcast_select_fusion, pred[]{:T(512)S(6)} %eq.22), kind=kLoop, calls=%fused_computation.5 | loop fusion | flops 37748736 | bytes 50331648 | tf_op jit(solution)/shard_map/jit(_where)/select_n | solution.py:14
  584.9 32.2 %copy.65 = bf16[2,128,128,384,1]{2,1,3,4,0:T(8,128)(2,1)} copy(bf16[2,128,128,384,1]{3,2,1,0,4:T(8,128)(2,1)} %fusion.2) | data formatting | bytes 50331648 | tf_op jit(solution)/shard_map/jit(_where)/select_n | solution.py:14
  617.1 27.3 %fusion.21 = f32[2,128,3,64]{1,3,2,0:T(8,128)S(1)} fusion(bf16[2,128,128,384,1]{2,1,3,4,0:T(8,128)(2,1)} %copy.65, bf16[2,3,64,128,384]{3,4,2,0,1:T(8,128)(2,1)} %pad_maximum_fusion), kind=kOutput, calls=%fused_computation.26 | convolution fusion | flops 4831838208 | bytes 63111168 | tf_op jit(solution)/shard_map/lqrc,loprc->lqop/dot_general | solution.py:127
  644.7 0.4 reshape.145
  645.1 7.4 %all_to_all.15 = f32[2,1,24576]{2,1,0:T(1,128)S(1)} all-to-all(f32[2,1,24576]{2,1,0:T(1,128)S(1)} %reshape.145), channel_id=1, replica_groups=mesh['atom'=16,'aux'=2] {'aux'}, dimensions={0} | all-to-all | bytes 393216 | tf_op jit(solution)/shard_map/all_to_all | solution.py:130
  652.5 0.5 broadcast.157
  653.0 1.2 reduce
  654.2 0.4 reshape.146
  654.6 0.3 copy.55
  654.9 1.0 reshape.136
  (40 shorter events, 1.9 us)
Async XLA Ops:
  6.9 289.5 %collective-permute-start.1 = (bf16[128,384]{1,0:T(8,128)(2,1)S(1)}, bf16[128,384]{1,0:T(8,128)(2,1)S(1)}, u32[]{:S(2)}, u32[]{:S(2)}) collective-permute-start(bf16[128,384]{1,0:T(8,128)(2,1)S(1)} %get-tuple-element.14), channel_id=1, source_target_pairs={{0,2},{2,4},{4,6},{6,8},{8,10},{10,12},{12,14},{14,16},{16,18},{18... | collective-permute-start | bytes 294920 | tf_op jit(solution)/shard_map/ppermute | solution.py:26
  7.0 289.4 %collective-permute-start.2 = (bf16[128,384]{1,0:T(8,128)(2,1)S(1)}, bf16[128,384]{1,0:T(8,128)(2,1)S(1)}, u32[]{:S(2)}, u32[]{:S(2)}) collective-permute-start(bf16[128,384]{1,0:T(8,128)(2,1)S(1)} %get-tuple-element.15), channel_id=1, source_target_pairs={{2,0},{4,2},{6,4},{8,6},{10,8},{12,10},{14,12},{16,14},{18,16},{20... | collective-permute-start | bytes 294920 | tf_op jit(solution)/shard_map/ppermute | solution.py:28
  21.7 538.3 %collective-permute-start = (bf16[2,64,128,384]{3,2,1,0:T(8,128)(2,1)}, bf16[2,64,128,384]{3,2,1,0:T(8,128)(2,1)}, u32[]{:S(2)}, u32[]{:S(2)}) collective-permute-start(bf16[2,64,128,384]{3,2,1,0:T(8,128)(2,1)} %broadcast_select_fusion), channel_id=1, source_target_pairs={{0,1},{1,0},{2,3},{3,2},{4,5},{5,4},{6,7},{7,6},{8,9},{9,8},{10,11... | collective-permute-start | bytes 37748744 | tf_op jit(solution)/shard_map/ppermute | solution.py:11
  23.2 14.1 %copy-start.1 = (bf16[128,384]{1,0:T(8,128)(2,1)S(1)}, bf16[128,384]{1,0:T(8,128)(2,1)}, u32[]{:S(2)}) copy-start(bf16[128,384]{1,0:T(8,128)(2,1)} %param.8) | copy-start | bytes 294916
  378.7 138.1 %collective-permute-start.3 = (bf16[64,128,384]{1,2,0:T(8,128)(2,1)}, bf16[64,128,384]{1,2,0:T(8,128)(2,1)}, u32[]{:S(2)}, u32[]{:S(2)}) collective-permute-start(bf16[64,128,384]{1,2,0:T(8,128)(2,1)} %get-tuple-element.8), channel_id=1, source_target_pairs={{0,2},{2,4},{4,6},{6,8},{8,10},{10,12},{12,14},{14,16},{16,18},{18... | collective-permute-start | bytes 18874376 | tf_op jit(solution)/shard_map/ppermute | solution.py:38
  389.3 127.5 %slice-start = ((s8[6291456]{0:T(1024)(128)(4,1)}), s8[2097152]{0:T(1024)(128)(4,1)S(1)}, s32[]{:S(2)}) async-start(s8[6291456]{0:T(1024)(128)(4,1)} %bitcast.82), calls=%async_computation.1 | async-start | bytes 4194304
  402.1 124.0 %collective-permute-start.4 = (bf16[64,128,384]{1,2,0:T(8,128)(2,1)}, bf16[64,128,384]{1,2,0:T(8,128)(2,1)}, u32[]{:S(2)}, u32[]{:S(2)}) collective-permute-start(bf16[64,128,384]{1,2,0:T(8,128)(2,1)} %get-tuple-element.11), channel_id=1, source_target_pairs={{0,30},{2,0},{4,2},{6,4},{8,6},{10,8},{12,10},{14,12},{16,14},{18,... | collective-permute-start | bytes 18874376 | tf_op jit(solution)/shard_map/ppermute | solution.py:38
  403.8 113.0 %slice-start.1 = ((s8[6291456]{0:T(1024)(128)(4,1)}), s8[4194304]{0:T(1024)(128)(4,1)S(1)}, s32[]{:S(2)}) async-start(s8[6291456]{0:T(1024)(128)(4,1)} %bitcast.82), calls=%async_computation.2 | async-start | bytes 8388608
  516.8 9.2 %copy-start = (bf16[1,64,128,384]{2,3,1,0:T(8,128)(2,1)S(1)}, bf16[1,64,128,384]{2,3,1,0:T(8,128)(2,1)}, u32[]{:S(2)}) copy-start(bf16[1,64,128,384]{2,3,1,0:T(8,128)(2,1)} %get-tuple-element.10) | copy-start | bytes 18874372
